TPU v7x, 128 devices: a whole 4x4x4 slice. The times are simulated.
128 devices in a mesh: member: 4 (over z), space: 32 (over x, y, core).
Axes of the slice: x: 4, y: 4, z: 4, core: 2. Of those that a mesh axis runs over, the one named last changes fastest.
Arguments:
- background: bfloat16 [80, 20, 65536], P('member', None, 'space'), may hold values from -6 to 6
- perturbation: bfloat16 [80, 524288], P(None, ('member', 'space')), may hold values from -0.875 to 0.875
- innovation: float32 [524288], P(('member', 'space')), may hold values from -6 to 6
- obs_weight: float32 [524288], P(('member', 'space')), may hold values from 0.5 to 4
- route_dest: int32 [524288, 2], P(('member', 'space')), may hold values from 0 to 127, all different within a row; in each aligned block of 4096 rows (0 to 4095, 4096 to 8191, ...) at most 128 rows name the same one
- localization: float32 [2, 1, 524288], P(None, None, ('member', 'space')), may hold values from 0.05 to 1
Outputs:
- analysis: bfloat16 [80, 20, 65536], P('member', None, 'space')
Inputs may be any that keep to these rules, and one draw needn't show every extreme that they name: `route_dest`: each observation names 2 different units. Within the rows of one device no unit is named by more than 128 rows, a bound that some block reaches.
All inputs are finite; a program needn't handle non-finite values.
Results may differ from a plain program's by a relative error of at most 0.0052.
Values may be sent and summed in bfloat16 or wider, within the bound.
A program may use at most 128 MiB of HBM per device.

v0:
```python
import math

import jax
import jax.numpy as jnp
from jax import lax
from jax.sharding import PartitionSpec as P

NS_ITERS = 16


def build_slots(perturbation, innovation, obs_weight, route_dest, localization, unit_count):
    obs_count, reach_count = route_dest.shape
    members = perturbation.shape[0]
    patches = localization.shape[1]
    entries = obs_count * reach_count
    capacity = 2 * entries // unit_count
    targets = route_dest.reshape(entries)
    unit_hot = (targets[:, None] == jnp.arange(unit_count, dtype=jnp.int32)[None, :]).astype(
        jnp.bfloat16
    )
    block_rows = math.gcd(entries, 512)
    block_count = entries // block_rows
    lower = (jnp.arange(block_rows)[:, None] > jnp.arange(block_rows)[None, :]).astype(jnp.bfloat16)
    hot_blocks = unit_hot.reshape(block_count, block_rows, unit_count)
    inside = jnp.einsum("ab,nbu->nau", lower, hot_blocks, preferred_element_type=jnp.float32)
    totals = jnp.sum(hot_blocks.astype(jnp.float32), axis=1)
    before = jnp.cumsum(totals, axis=0) - totals
    rank_all = (inside + before[:, None, :]).reshape(entries, unit_count)
    rank = jnp.sum(rank_all * unit_hot.astype(jnp.float32), axis=1)
    rank_hot = (rank[:, None] == jnp.arange(capacity, dtype=jnp.float32)[None, :]).astype(
        jnp.bfloat16
    )
    col_entries = jnp.broadcast_to(
        perturbation[:, :, None], (members, obs_count, reach_count)
    ).reshape(members, entries)
    scaled = obs_weight[None, :, None] * jnp.transpose(localization, (1, 2, 0))
    coef = scaled.reshape(patches, entries).astype(jnp.bfloat16)
    weighted = (scaled * innovation[None, :, None]).reshape(patches, entries).astype(jnp.bfloat16)
    stacked = jnp.concatenate([col_entries, coef, weighted], axis=0)
    group = math.gcd(unit_count, 8)
    unit_major = unit_hot.T.reshape(unit_count // group, group, entries)

    def place(hot):
        masked = stacked[None, :, :] * hot[:, None, :]
        return jnp.einsum(
            "gre,ec->grc", masked, rank_hot, preferred_element_type=jnp.float32
        ).astype(jnp.bfloat16)

    placed = lax.map(place, unit_major)
    row_total = stacked.shape[0]
    placed = jnp.transpose(placed.reshape(unit_count, row_total, capacity), (1, 0, 2)).reshape(
        row_total, unit_count * capacity
    )
    return (placed[:members], placed[members:], capacity)


def local_gram(arrived_cols, arrived_wts, patches):
    column_vals = arrived_cols.astype(jnp.float32)
    weight_vals = arrived_wts.astype(jnp.float32)
    gram_sum = jnp.einsum(
        "ks,ps,ls->pkl",
        column_vals,
        weight_vals[:patches],
        column_vals,
        precision=lax.Precision.HIGHEST,
    )
    right_side = jnp.einsum(
        "ks,ps->pk", column_vals, weight_vals[patches:], precision=lax.Precision.HIGHEST
    )
    return (gram_sum, right_side)


def transform(gram_sum, right_side, members, steps_count):
    identity = jnp.eye(members, dtype=jnp.float32)
    system = gram_sum + (members - 1.0) * identity
    scale = jnp.linalg.norm(system, axis=(-2, -1))[..., None, None]
    start_pair = (system / scale, jnp.broadcast_to(identity, system.shape))

    def newton_step(index, pair):
        approx, inverse = pair
        half = 0.5 * (3.0 * identity - jnp.matmul(inverse, approx, precision=lax.Precision.HIGHEST))
        approx = jnp.matmul(approx, half, precision=lax.Precision.HIGHEST)
        inverse = jnp.matmul(half, inverse, precision=lax.Precision.HIGHEST)
        return (approx, inverse)

    final_pair = lax.fori_loop(0, steps_count, newton_step, start_pair)
    inverse_root = final_pair[1] / jnp.sqrt(scale)
    halfway = jnp.matmul(inverse_root, right_side[..., :, None], precision=lax.Precision.HIGHEST)
    mean_weights = jnp.matmul(inverse_root, halfway, precision=lax.Precision.HIGHEST)[..., 0]
    weights = mean_weights[..., :, None] + math.sqrt(members - 1.0) * inverse_root
    column_sum = jnp.sum(weights, axis=-2, keepdims=True)
    mixing = weights + (1.0 - column_sum) / members
    return mixing.astype(jnp.bfloat16)


def per_device(background, perturbation, innovation, obs_weight, route_dest, localization):
    member_groups = lax.axis_size("member")
    space_groups = lax.axis_size("space")
    unit_count = member_groups * space_groups
    members = perturbation.shape[0]
    patches = localization.shape[1]
    local_state = lax.all_to_all(background, "member", split_axis=2, concat_axis=0, tiled=True)
    columns, weights, capacity = build_slots(
        perturbation, innovation, obs_weight, route_dest, localization, unit_count
    )
    arrived_cols, arrived_wts = (
        lax.all_to_all(columns, ("member", "space"), split_axis=1, concat_axis=1, tiled=True),
        lax.all_to_all(weights, ("member", "space"), split_axis=1, concat_axis=1, tiled=True),
    )
    gram_sum, right_side = local_gram(arrived_cols, arrived_wts, patches)
    mixing = transform(gram_sum, right_side, members, NS_ITERS)
    state_blocks = local_state.reshape(members, local_state.shape[1], patches, -1)
    analysed = jnp.einsum(
        "jfpi,pjk->kfpi", state_blocks, mixing, preferred_element_type=jnp.float32
    )
    analysed = analysed.astype(jnp.bfloat16).reshape(local_state.shape)
    return lax.all_to_all(analysed, "member", split_axis=0, concat_axis=2, tiled=True)


def solution(mesh):
    in_specs = (
        P("member", None, "space"),
        P(None, ("member", "space")),
        P(("member", "space")),
        P(("member", "space")),
        P(("member", "space"), None),
        P(None, None, ("member", "space")),
    )
    out_specs = P("member", None, "space")
    return jax.shard_map(
        per_device, mesh=mesh, in_specs=in_specs, out_specs=out_specs, check_vma=False
    )
```

profile of v0, /device:TPU:0, one launch (start us, length us, event | category | flops | bytes accessed | tf_op | source)
XLA Modules:
  0.0 263.4 jit_solution(12382736777714274902)
XLA Ops:
  22.9 75.6 %while.24 = (s32[]{:T(128)}, bf16[16,8,82,128]{3,2,1,0:T(8,128)(2,1)}, bf16[82,8192]{1,0:T(8,128)(2,1)S(1)}, bf16[16,8,8192]{2,1,0:T(8,128)(2,1)S(1)}, f32[8192]{0:T(1024)}, /*index=5*/s32[]{:T(128)}) while((s32[]{:T(128)}, bf16[16,8,82,128]{3,2,1,0:T(8,128)(2,1)}, bf16[82,8192]{1,0:T(8,128)(2,1)S(1)}, ...), condition=%wide.region_4.5_spmd.clone, body=%wide.region_3.4_spmd.clone.sunk | while | flops 1383286784 | bytes 1949781 | solution.py:49
  22.9 4.7 %fusion.86 = bf16[16,8,82,128]{3,2,1,0:T(8,128)(2,1)} fusion(bf16[16,8,82,128]{3,2,1,0:T(8,128)(2,1)} %get-tuple-element.183, s32[]{:T(128)S(6)} %copy.87, f32[8192]{0:T(1024)} %get-tuple-element.192, bf16[8,8192]{1,0:T(8,128)(2,1)S(1)} %dynamic-slice_bitcast_fusion.2, bf16[82,8192]{1,0:T(8,128)(2,1)S(1)} %get-tuple-element.190), kind=kOutput, calls=%fused_computation.12.clone.1 | convolution fusion | flops 1383286784 | bytes 1687556 | tf_op jit(solution)/shard_map/while/body/eval_jaxpr/gre,ec->grc/dot_general | solution.py:45
  27.6 4.7 %fusion.86 = bf16[16,8,82,128]{3,2,1,0:T(8,128)(2,1)} fusion(bf16[16,8,82,128]{3,2,1,0:T(8,128)(2,1)} %get-tuple-element.183, s32[]{:T(128)S(6)} %copy.87, f32[8192]{0:T(1024)} %get-tuple-element.192, bf16[8,8192]{1,0:T(8,128)(2,1)S(1)} %dynamic-slice_bitcast_fusion.2, bf16[82,8192]{1,0:T(8,128)(2,1)S(1)} %get-tuple-element.190), kind=kOutput, calls=%fused_computation.12.clone.1 | convolution fusion | flops 1383286784 | bytes 1687556 | tf_op jit(solution)/shard_map/while/body/eval_jaxpr/gre,ec->grc/dot_general | solution.py:45
  32.3 4.7 %fusion.86 = bf16[16,8,82,128]{3,2,1,0:T(8,128)(2,1)} fusion(bf16[16,8,82,128]{3,2,1,0:T(8,128)(2,1)} %get-tuple-element.183, s32[]{:T(128)S(6)} %copy.87, f32[8192]{0:T(1024)} %get-tuple-element.192, bf16[8,8192]{1,0:T(8,128)(2,1)S(1)} %dynamic-slice_bitcast_fusion.2, bf16[82,8192]{1,0:T(8,128)(2,1)S(1)} %get-tuple-element.190), kind=kOutput, calls=%fused_computation.12.clone.1 | convolution fusion | flops 1383286784 | bytes 1687556 | tf_op jit(solution)/shard_map/while/body/eval_jaxpr/gre,ec->grc/dot_general | solution.py:45
  37.1 4.7 %fusion.86 = bf16[16,8,82,128]{3,2,1,0:T(8,128)(2,1)} fusion(bf16[16,8,82,128]{3,2,1,0:T(8,128)(2,1)} %get-tuple-element.183, s32[]{:T(128)S(6)} %copy.87, f32[8192]{0:T(1024)} %get-tuple-element.192, bf16[8,8192]{1,0:T(8,128)(2,1)S(1)} %dynamic-slice_bitcast_fusion.2, bf16[82,8192]{1,0:T(8,128)(2,1)S(1)} %get-tuple-element.190), kind=kOutput, calls=%fused_computation.12.clone.1 | convolution fusion | flops 1383286784 | bytes 1687556 | tf_op jit(solution)/shard_map/while/body/eval_jaxpr/gre,ec->grc/dot_general | solution.py:45
  41.8 4.7 %fusion.86 = bf16[16,8,82,128]{3,2,1,0:T(8,128)(2,1)} fusion(bf16[16,8,82,128]{3,2,1,0:T(8,128)(2,1)} %get-tuple-element.183, s32[]{:T(128)S(6)} %copy.87, f32[8192]{0:T(1024)} %get-tuple-element.192, bf16[8,8192]{1,0:T(8,128)(2,1)S(1)} %dynamic-slice_bitcast_fusion.2, bf16[82,8192]{1,0:T(8,128)(2,1)S(1)} %get-tuple-element.190), kind=kOutput, calls=%fused_computation.12.clone.1 | convolution fusion | flops 1383286784 | bytes 1687556 | tf_op jit(solution)/shard_map/while/body/eval_jaxpr/gre,ec->grc/dot_general | solution.py:45
  51.3 4.7 %fusion.86 = bf16[16,8,82,128]{3,2,1,0:T(8,128)(2,1)} fusion(bf16[16,8,82,128]{3,2,1,0:T(8,128)(2,1)} %get-tuple-element.183, s32[]{:T(128)S(6)} %copy.87, f32[8192]{0:T(1024)} %get-tuple-element.192, bf16[8,8192]{1,0:T(8,128)(2,1)S(1)} %dynamic-slice_bitcast_fusion.2, bf16[82,8192]{1,0:T(8,128)(2,1)S(1)} %get-tuple-element.190), kind=kOutput, calls=%fused_computation.12.clone.1 | convolution fusion | flops 1383286784 | bytes 1687556 | tf_op jit(solution)/shard_map/while/body/eval_jaxpr/gre,ec->grc/dot_general | solution.py:45
  60.7 4.7 %fusion.86 = bf16[16,8,82,128]{3,2,1,0:T(8,128)(2,1)} fusion(bf16[16,8,82,128]{3,2,1,0:T(8,128)(2,1)} %get-tuple-element.183, s32[]{:T(128)S(6)} %copy.87, f32[8192]{0:T(1024)} %get-tuple-element.192, bf16[8,8192]{1,0:T(8,128)(2,1)S(1)} %dynamic-slice_bitcast_fusion.2, bf16[82,8192]{1,0:T(8,128)(2,1)S(1)} %get-tuple-element.190), kind=kOutput, calls=%fused_computation.12.clone.1 | convolution fusion | flops 1383286784 | bytes 1687556 | tf_op jit(solution)/shard_map/while/body/eval_jaxpr/gre,ec->grc/dot_general | solution.py:45
  70.1 4.7 %fusion.86 = bf16[16,8,82,128]{3,2,1,0:T(8,128)(2,1)} fusion(bf16[16,8,82,128]{3,2,1,0:T(8,128)(2,1)} %get-tuple-element.183, s32[]{:T(128)S(6)} %copy.87, f32[8192]{0:T(1024)} %get-tuple-element.192, bf16[8,8192]{1,0:T(8,128)(2,1)S(1)} %dynamic-slice_bitcast_fusion.2, bf16[82,8192]{1,0:T(8,128)(2,1)S(1)} %get-tuple-element.190), kind=kOutput, calls=%fused_computation.12.clone.1 | convolution fusion | flops 1383286784 | bytes 1687556 | tf_op jit(solution)/shard_map/while/body/eval_jaxpr/gre,ec->grc/dot_general | solution.py:45
  79.6 4.7 %fusion.86 = bf16[16,8,82,128]{3,2,1,0:T(8,128)(2,1)} fusion(bf16[16,8,82,128]{3,2,1,0:T(8,128)(2,1)} %get-tuple-element.183, s32[]{:T(128)S(6)} %copy.87, f32[8192]{0:T(1024)} %get-tuple-element.192, bf16[8,8192]{1,0:T(8,128)(2,1)S(1)} %dynamic-slice_bitcast_fusion.2, bf16[82,8192]{1,0:T(8,128)(2,1)S(1)} %get-tuple-element.190), kind=kOutput, calls=%fused_computation.12.clone.1 | convolution fusion | flops 1383286784 | bytes 1687556 | tf_op jit(solution)/shard_map/while/body/eval_jaxpr/gre,ec->grc/dot_general | solution.py:45
  84.3 4.7 %fusion.86 = bf16[16,8,82,128]{3,2,1,0:T(8,128)(2,1)} fusion(bf16[16,8,82,128]{3,2,1,0:T(8,128)(2,1)} %get-tuple-element.183, s32[]{:T(128)S(6)} %copy.87, f32[8192]{0:T(1024)} %get-tuple-element.192, bf16[8,8192]{1,0:T(8,128)(2,1)S(1)} %dynamic-slice_bitcast_fusion.2, bf16[82,8192]{1,0:T(8,128)(2,1)S(1)} %get-tuple-element.190), kind=kOutput, calls=%fused_computation.12.clone.1 | convolution fusion | flops 1383286784 | bytes 1687556 | tf_op jit(solution)/shard_map/while/body/eval_jaxpr/gre,ec->grc/dot_general | solution.py:45
  89.0 4.7 %fusion.86 = bf16[16,8,82,128]{3,2,1,0:T(8,128)(2,1)} fusion(bf16[16,8,82,128]{3,2,1,0:T(8,128)(2,1)} %get-tuple-element.183, s32[]{:T(128)S(6)} %copy.87, f32[8192]{0:T(1024)} %get-tuple-element.192, bf16[8,8192]{1,0:T(8,128)(2,1)S(1)} %dynamic-slice_bitcast_fusion.2, bf16[82,8192]{1,0:T(8,128)(2,1)S(1)} %get-tuple-element.190), kind=kOutput, calls=%fused_computation.12.clone.1 | convolution fusion | flops 1383286784 | bytes 1687556 | tf_op jit(solution)/shard_map/while/body/eval_jaxpr/gre,ec->grc/dot_general | solution.py:45
  93.8 4.7 %fusion.86 = bf16[16,8,82,128]{3,2,1,0:T(8,128)(2,1)} fusion(bf16[16,8,82,128]{3,2,1,0:T(8,128)(2,1)} %get-tuple-element.183, s32[]{:T(128)S(6)} %copy.87, f32[8192]{0:T(1024)} %get-tuple-element.192, bf16[8,8192]{1,0:T(8,128)(2,1)S(1)} %dynamic-slice_bitcast_fusion.2, bf16[82,8192]{1,0:T(8,128)(2,1)S(1)} %get-tuple-element.190), kind=kOutput, calls=%fused_computation.12.clone.1 | convolution fusion | flops 1383286784 | bytes 1687556 | tf_op jit(solution)/shard_map/while/body/eval_jaxpr/gre,ec->grc/dot_general | solution.py:45
  100.1 11.4 %all-to-all-start = ((bf16[2,128,128]{2,0,1:T(2,128)(2,1)}), bf16[2,128,128]{2,0,1:T(2,128)(2,1)S(1)}, u32[]{:S(2)}, u32[]{:S(2)}) async-start(bf16[2,128,128]{2,0,1:T(2,128)(2,1)} %slice.20), calls=%async_computation | async-start | bytes 131072 | tf_op jit(solution)/shard_map/all_to_all | solution.py:108
  111.5 13.1 %copy.49 = bf16[20,20,2048]{1,0,2:T(8,128)(2,1)} copy(bf16[20,20,2048]{2,1,0:T(8,128)(2,1)} %param.10) | data formatting | bytes 3276800 | tf_op args[0]
  124.5 15.9 %reshape.209 = bf16[4,2,102400]{2,1,0:T(2,128)(2,1)} reshape(bf16[2048,20,20]{2,1,0:T(8,128)(2,1)} %bitcast.135) | data formatting | bytes 3276800
  147.7 18.4 %all-to-all-done.2 = bf16[4,2,102400]{2,1,0:T(2,128)(2,1)S(1)} async-done(((bf16[4,2,102400]{2,1,0:T(2,128)(2,1)}), bf16[4,2,102400]{2,1,0:T(2,128)(2,1)S(1)}, u32[]{:S(2)}, u32[]{:S(2)}) %all-to-all-start.2) | async-done | bytes 1638432 | tf_op jit(solution)/shard_map/all_to_all | solution.py:102
  166.1 8.5 %all-to-all-start.1 = ((bf16[80,128,128]{2,0,1:T(8,128)(2,1)}), bf16[80,128,128]{2,0,1:T(8,128)(2,1)}, u32[]{:S(2)}, u32[]{:S(2)}) async-start(bf16[80,128,128]{2,0,1:T(8,128)(2,1)} %slice.22), calls=%async_computation.1 | async-start | bytes 5242880 | tf_op jit(solution)/shard_map/all_to_all | solution.py:107
  174.8 14.5 %reshape.210 = bf16[2048,20,20]{2,1,0:T(8,128)(2,1)} reshape(bf16[4,2,102400]{2,1,0:T(2,128)(2,1)S(1)} %all-to-all-done.2) | data formatting | bytes 3276800
  189.3 13.7 %copy.50 = bf16[20,20,4,512]{3,0,2,1:T(8,128)(2,1)S(1)} copy(bf16[20,20,4,512]{1,0,3,2:T(8,128)(2,1)} %bitcast.134) | data formatting | bytes 3276800 | tf_op jit(solution)/shard_map/all_to_all | solution.py:102
  204.4 5.9 %all-to-all-done.1 = bf16[80,128,128]{2,0,1:T(8,128)(2,1)} async-done(((bf16[80,128,128]{2,0,1:T(8,128)(2,1)}), bf16[80,128,128]{2,0,1:T(8,128)(2,1)}, u32[]{:S(2)}, u32[]{:S(2)}) %all-to-all-start.1) | async-done | bytes 2621472 | tf_op jit(solution)/shard_map/all_to_all | solution.py:107
  210.3 6.0 %multiply_reduce_fusion = (f32[]{:T(128)}, f32[80,80]{1,0:T(8,128)S(1)}) fusion(f32[16384]{0:T(1024)S(1)} %bitcast.142, bf16[80,128,128]{2,0,1:T(8,128)(2,1)} %all-to-all-done.1), kind=kOutput, calls=%fused_computation.55 | convolution fusion | flops 1260944640 | bytes 2712580 | tf_op jit(solution)/shard_map/ks,ps,ls->pkl/dot_general | solution.py:60
  217.1 11.0 %while.25 = (s32[]{:T(128)}, f32[1,80,80]{1,2,0:T(8,128)S(1)}, f32[1,80,80]{2,1,0:T(8,128)S(1)}, s32[]{:T(128)}) while((s32[]{:T(128)}, f32[1,80,80]{1,2,0:T(8,128)S(1)}, f32[1,80,80]{2,1,0:T(8,128)S(1)}, s32[]{:T(128)}) %tuple.50), condition=%wide.region_7.8_spmd.clone, body=%wide.region_6.7_spmd.clone.sunk | while | flops 18457600 | bytes 332853 | solution.py:86
  232.7 27.4 %all_to_all.48 = bf16[80,20,512]{2,1,0:T(8,128)(2,1)S(1)} all-to-all(bf16[80,20,512]{2,1,0:T(8,128)(2,1)S(1)} %copy.52), channel_id=1, replica_groups=mesh['member'=4,'space'=32] {'member'}, dimensions={0} | all-to-all | bytes 3276800 | tf_op jit(solution)/shard_map/all_to_all | solution.py:117
  (154 shorter events, 70.1 us)
Async XLA Ops:
  1.4 3.7 %copy-start.4 = (f32[2,1,4096]{2,1,0:T(1,128)S(1)}, f32[2,1,4096]{2,1,0:T(1,128)}, u32[]{:S(2)}) copy-start(f32[2,1,4096]{2,1,0:T(1,128)} %param.15) | copy-start | bytes 98308
  1.4 3.7 %copy-start.5 = (f32[4096]{0:T(1024)S(1)}, f32[4096]{0:T(1024)}, u32[]{:S(2)}) copy-start(f32[4096]{0:T(1024)} %param.13) | copy-start | bytes 49156
  1.4 3.7 %copy-start.6 = (f32[4096]{0:T(1024)S(1)}, f32[4096]{0:T(1024)}, u32[]{:S(2)}) copy-start(f32[4096]{0:T(1024)} %param.12) | copy-start | bytes 49156
  7.7 2.4 copy-start.2
  10.7 1.6 copy-start
  19.1 3.3 %copy-start.3 = (s32[8192]{0:T(1024)S(1)}, s32[8192]{0:T(1024)}, u32[]{:S(2)}) copy-start(s32[8192]{0:T(1024)} %eq.63) | copy-start | bytes 98308
  100.1 40.3 %all-to-all-start = ((bf16[2,128,128]{2,0,1:T(2,128)(2,1)}), bf16[2,128,128]{2,0,1:T(2,128)(2,1)S(1)}, u32[]{:S(2)}, u32[]{:S(2)}) async-start(bf16[2,128,128]{2,0,1:T(2,128)(2,1)} %slice.20), calls=%async_computation | async-start | bytes 131072 | tf_op jit(solution)/shard_map/all_to_all | solution.py:108
  140.4 25.6 %all-to-all-start.2 = ((bf16[4,2,102400]{2,1,0:T(2,128)(2,1)}), bf16[4,2,102400]{2,1,0:T(2,128)(2,1)S(1)}, u32[]{:S(2)}, u32[]{:S(2)}) async-start(bf16[4,2,102400]{2,1,0:T(2,128)(2,1)} %reshape.209), calls=%async_computation.2 | async-start | bytes 3276800 | tf_op jit(solution)/shard_map/all_to_all | solution.py:102
  166.1 44.2 %all-to-all-start.1 = ((bf16[80,128,128]{2,0,1:T(8,128)(2,1)}), bf16[80,128,128]{2,0,1:T(8,128)(2,1)}, u32[]{:S(2)}, u32[]{:S(2)}) async-start(bf16[80,128,128]{2,0,1:T(8,128)(2,1)} %slice.22), calls=%async_computation.1 | async-start | bytes 5242880 | tf_op jit(solution)/shard_map/all_to_all | solution.py:107
  217.1 14.0 %copy-start.1 = (bf16[80,20,512]{2,0,1:T(8,128)(2,1)S(1)}, bf16[80,20,512]{2,0,1:T(8,128)(2,1)}, u32[]{:S(2)}) copy-start(bf16[80,20,512]{2,0,1:T(8,128)(2,1)} %reshape.198) | copy-start | bytes 4915204
where the time goes:
time: 266 us; the launch traced here: 263 us
  matrix products  97.7 us (37%)
  local copies, waits for them, and re-layouts  82.9 us (31%)
  blocking collectives  27.4 us (10%)
  waiting for transfers between devices  24.3 us (9%)
  starting transfers between devices  23.8 us (9%)
  other arithmetic  5.53 us (2%)
    dot_general x16, matrix products, place(): jnp.einsum('gre,ec->grc', masked, rank_hot, preferred_element_type=jnp.fl...  75.4 us
    unnamed x23, local copies, waits for them, and re-layouts  48.6 us
    all_to_all x1, blocking collectives, per_device(): lax.all_to_all(analysed, 'member', split_axis=0, concat_axis=2, tiled=True)  27.4 us
    all_to_all x1, waiting for transfers between devices, per_device(): lax.all_to_all(background, 'member', split_axis=2, concat_axis=0, tiled=T...  18.4 us
    all_to_all x1, local copies, waits for them, and re-layouts, per_device(): lax.all_to_all(background, 'member', split_axis=2, concat_axis=0, tiled=T...  13.7 us
    all_to_all x1, starting transfers between devices, per_device(): lax.all_to_all(weights, ('member', 'space'), split_axis=1, concat_axis=1,...  11.4 us
    all_to_all x1, starting transfers between devices, per_device(): lax.all_to_all(columns, ('member', 'space'), split_axis=1, concat_axis=1,...  8.54 us
    dot_general x1, matrix products, local_gram(): jnp.einsum('ks,ps,ls->pkl', column_vals, weight_vals[:patches], column_va...  6.05 us
  transfers between devices with their start and end apart: 3, of which 2 were waited for; matrix products, arithmetic and copies ran while one was open for 24% of the time, Pallas kernels for 0%

commit v1 on v0

v1 whole, which is shorter than its diff:
```python
import math

import jax
import jax.numpy as jnp
from jax import lax
from jax.experimental import pallas as pl
from jax.experimental.pallas import tpu as pltpu
from jax.sharding import PartitionSpec as P

BF = jnp.bfloat16
F32 = jnp.float32
MESH = pl.DeviceIdType.MESH
NN = (((1,), (0,)), ((), ()))
NT = (((1,), (1,)), ((), ()))

K = 80
OBS = 4096
UNITS = 128
Z = 4
XY = 16
FL = 20
FQ = 5
PATCH = 512
NS_STEPS = 8

GROUPS = (
    ((0, 0, 80), (32, 32, 48)),
    ((8, 8, 72), (24, 24, 56)),
    ((16, 16, 64), (40, 40, 40), (56, 56, 24)),
    ((48, 48, 32), (64, 64, 16), (72, 72, 8)),
)
NG = len(GROUPS)
WIDTH = tuple(sum(n for _, _, n in blocks) for blocks in GROUPS)
RHS_LANE = WIDTH[-1]


def iota(shape, dim):
    return lax.broadcasted_iota(jnp.int32, shape, dim)


def dot(a, b, dims=NN, precision=None):
    return lax.dot_general(a, b, dims, preferred_element_type=F32, precision=precision)


def dot_exact(a, b):
    return dot(a, b, precision=lax.Precision.HIGHEST)


def build_weights(dest, weight, innovation, localization, coef, weighted):
    step = 512
    row = iota((UNITS, 1), 0)
    unit = (row % Z) * 32 + ((row % 64) // Z) * 2 + row // 64
    for start in range(0, OBS, step):
        at = slice(start, start + step)
        first = weight[:, at] * localization[0, :, at]
        second = weight[:, at] * localization[1, :, at]
        to_first = dest[0:1, at] == unit
        to_second = dest[1:2, at] == unit

        def pick(a, b):
            a, b = a.astype(BF).astype(F32), b.astype(BF).astype(F32)
            return jnp.where(to_first, a, jnp.where(to_second, b, 0.0)).astype(BF)

        coef[:, at] = pick(first, second)
        weighted[:, at] = pick(first * innovation[:, at], second * innovation[:, at])


def build_products(y, feats, group):
    step = 512
    for start in range(0, OBS, step):
        at = slice(start, start + step)
        row = 0
        for i in range(8):
            for k, l, n in GROUPS[group]:
                feats[row : row + n, at] = y[k + i : k + i + 1, at] * y[l : l + n, at]
                row += n


def inverse_root(system):
    eye = (iota((K, K), 0) == iota((K, K), 1)).astype(F32)
    upper = jnp.max(jnp.sum(jnp.abs(system), axis=1, keepdims=True), axis=0, keepdims=True)
    low = jnp.sqrt((K - 1.0) / upper)
    approx, inverse = system * (1.0 / upper), None
    for step in range(NS_STEPS):
        square = 3.0 / (1.0 + low + low * low)
        stretch = jnp.sqrt(square)
        product = approx if inverse is None else dot_exact(inverse, approx)
        half = (1.5 * stretch) * eye - (0.5 * stretch * square) * product
        low = 0.5 * stretch * low * (3.0 - square * low * low)
        if step < NS_STEPS - 1:
            approx = dot_exact(approx, half)
        inverse = half if inverse is None else dot_exact(half, inverse)
    return inverse * lax.rsqrt(upper)


def unpack_system(total):
    lane = iota((8, 128), 1)
    tiles = [None] * (K // 8)
    for g, blocks in enumerate(GROUPS):
        slots = total[8 * g : 8 * g + 8]
        offset = 0
        for k, l, n in blocks:
            rolled = pltpu.roll(slots, (l - offset) % 128, 1) if l != offset else slots
            tiles[k // 8] = jnp.where((lane >= l) & (lane < l + n), rolled, 0.0)
            offset += n
    upper = jnp.concatenate(tiles + [jnp.zeros((128 - K, 128), F32)], axis=0)
    row, col = iota((128, 128), 0), iota((128, 128), 1)
    above = jnp.where((row // 8) == (col // 8), 0.0, upper)
    gram = (upper + above.T)[:K, :K]
    eye = (iota((K, K), 0) == iota((K, K), 1)).astype(F32)
    slots = total[8 * (NG - 1) :]
    part = jnp.zeros((8, 128), F32)
    for i in range(K // 16):
        rolled = pltpu.roll(slots, (16 * i - RHS_LANE) % 128, 1)
        part = jnp.where((iota((8, 128), 0) == i) & (lane // 16 == i), rolled, part)
    right_side = jnp.sum(part, axis=0, keepdims=True)[:, :K]
    return gram + (K - 1.0) * eye, right_side


def mixing_t(root, right_side):
    halfway = jnp.sum(root * right_side, axis=1, keepdims=True)
    mean = jnp.sum(root * halfway, axis=0, keepdims=True)
    spread = math.sqrt(K - 1.0) * root
    column = jnp.sum(mean, axis=1, keepdims=True) + jnp.sum(spread, axis=1, keepdims=True)
    return (mean + spread + (1.0 - column) / K).astype(BF)


def kernel(
    bg, y_in, dest_in, weight_in, innovation_in, local_in, out,
    bgv, y, dest, weight, innovation, local, coef, weighted, feats, gbuf, gpeer,
    stage, stage16, plane, zsend, zrecv, prep, land, back, back_land,
    in_sem, core_s, core_r, plane_s, plane_r, z_s, z_r, bg_s, bg_r, back_s, back_r,
):
    z = lax.axis_index("member")
    s = lax.axis_index("space")
    core = lax.rem(s, 2)
    xy = lax.div(s, 2)

    def z_peer(d):
        return (lax.rem(z + d, Z), s)

    def plane_peer(d):
        return (z, 2 * lax.rem(xy + d, XY) + core)

    core_peer = (z, 2 * xy + 1 - core)

    barrier = pltpu.get_barrier_semaphore()
    for d in range(1, Z):
        pl.semaphore_signal(barrier, inc=1, device_id=z_peer(d), device_id_type=MESH)
    pl.semaphore_signal(barrier, inc=1, device_id=core_peer, device_id_type=MESH)
    for d in range(1, XY):
        pl.semaphore_signal(barrier, inc=1, device_id=plane_peer(d), device_id_type=MESH)

    loads = [
        pltpu.make_async_copy(src, dst, in_sem.at[i])
        for i, (src, dst) in enumerate(
            ((dest_in, dest), (weight_in, weight), (local_in, local), (innovation_in, innovation), (y_in, y), (bg, bgv))
        )
    ]
    for load in loads:
        load.start()

    def bg_copy(fq, d):
        return pltpu.make_async_remote_copy(
            prep.at[fq, d - 1], land.at[fq, z], bg_s.at[fq, d - 1], bg_r.at[fq, z], device_id=z_peer(d), device_id_type=MESH
        )

    def bg_arrival(fq, d):
        source = lax.rem(z + d, Z)
        return pltpu.make_async_remote_copy(
            prep.at[fq, d - 1], land.at[fq, source], bg_s.at[fq, d - 1], bg_r.at[fq, source], device_id=z_peer(d), device_id_type=MESH
        )

    def send_bg(fq):
        for d in (2, 1, 3):
            bg_copy(fq, d).start()

    def core_copy(g):
        return pltpu.make_async_remote_copy(
            gbuf.at[g, 1 - core], gpeer.at[g], core_s.at[g], core_r.at[g], device_id=core_peer, device_id_type=MESH
        )

    def plane_copy(g, d):
        return pltpu.make_async_remote_copy(
            stage16.at[g, lax.rem(xy + d, XY)], plane.at[g, xy], plane_s.at[g, d], plane_r.at[g, xy],
            device_id=plane_peer(d), device_id_type=MESH,
        )

    def plane_arrival(g, d):
        source = lax.rem(xy + d, XY)
        return pltpu.make_async_remote_copy(
            stage16.at[g, source], plane.at[g, source], plane_s.at[g, d], plane_r.at[g, source],
            device_id=plane_peer(d), device_id_type=MESH,
        )

    def z_copy(d):
        return pltpu.make_async_remote_copy(
            zsend.at[lax.rem(z + d, Z)], zrecv.at[z], z_s.at[d], z_r.at[z], device_id=z_peer(d), device_id_type=MESH
        )

    def z_arrival(d):
        source = lax.rem(z + d, Z)
        return pltpu.make_async_remote_copy(
            zsend.at[source], zrecv.at[source], z_s.at[d], z_r.at[source], device_id=z_peer(d), device_id_type=MESH
        )

    def back_copy(fq, d):
        return pltpu.make_async_remote_copy(
            back.at[fq, lax.rem(z + d, Z)], back_land.at[fq, z], back_s.at[fq, d - 1], back_r.at[fq, z],
            device_id=z_peer(d), device_id_type=MESH,
        )

    def back_arrival(fq, d):
        source = lax.rem(z + d, Z)
        return pltpu.make_async_remote_copy(
            back.at[fq, source], back_land.at[fq, source], back_s.at[fq, d - 1], back_r.at[fq, source],
            device_id=z_peer(d), device_id_type=MESH,
        )

    def partial_gram(g):
        width = WIDTH[g]
        buf = feats.at[g % 2]
        build_products(y, buf, g)
        tail = None
        if g == NG - 1:
            tail = dot(y[...], weighted[...], NT)
        for part in range(2):
            rows = 4 * width
            result = dot(buf[part * rows : (part + 1) * rows, :], coef[...], NT)
            for j in range(4):
                i = 4 * part + j
                slot = result[j * width : (j + 1) * width]
                if width < 128:
                    pieces = [slot]
                    filled = width
                    if i < K // 16:
                        pieces.append(tail[16 * i : 16 * i + 16])
                        filled += 16
                    pieces.append(jnp.zeros((128 - filled, UNITS), F32))
                    slot = jnp.concatenate(pieces, axis=0)
                turned = slot.T
                gbuf[g, 0, i] = turned[:64]
                gbuf[g, 1, i] = turned[64:]

    def send_plane(g):
        core_copy(g).wait_recv()
        for i in range(8):
            stage[g, pl.ds(i, 64, stride=8), :] = gbuf[g, core, i] + gpeer[g, i]
        stage16[g] = stage[g].reshape(XY, 32, 128).astype(BF)

        def start(d, carry):
            plane_copy(g, d).start()
            return carry

        lax.fori_loop(1, XY, start, 0)

    def sum_plane(g):
        def wait(d, carry):
            plane_arrival(g, d).wait_recv()
            return carry

        lax.fori_loop(1, XY, wait, 0)
        total = stage[g, pl.ds(pl.multiple_of(xy * 32, 32), 32), :]
        for d in range(1, XY):
            total = total + plane[g, lax.rem(xy + d, XY)].astype(F32)
        for t in range(Z):
            zsend[t, 8 * g : 8 * g + 8] = total[8 * t : 8 * t + 8]

    for load in loads[:5]:
        load.wait()
    build_weights(dest, weight, innovation, local, coef, weighted)
    partial_gram(0)

    loads[5].wait()
    for fq in range(FQ):
        rows = slice(4 * fq, 4 * fq + 4)
        for j in range(FL):
            to = slice(4 * j, 4 * j + 4)
            land[fq, z, to] = bgv[j, rows, pl.ds(pl.multiple_of(z * PATCH, PATCH), PATCH)]
            for d in range(1, Z):
                cells = pl.ds(pl.multiple_of(lax.rem(z + d, Z) * PATCH, PATCH), PATCH)
                prep[fq, d - 1, to] = bgv[j, rows, cells]

    pl.semaphore_wait(barrier, Z - 1 + 1 + XY - 1)
    core_copy(0).start()
    for fq in range(3):
        send_bg(fq)
    partial_gram(1)
    core_copy(1).start()
    send_plane(0)
    partial_gram(2)
    core_copy(2).start()
    send_plane(1)
    partial_gram(3)
    core_copy(3).start()
    send_plane(2)
    send_plane(3)
    expand = ((iota((4 * K, K), 0) // 4) == iota((4 * K, K), 1)).astype(BF)
    expand_t = (iota((K, 4 * K), 0) == (iota((K, 4 * K), 1) // 4)).astype(BF)
    for g in range(NG):
        sum_plane(g)
    for d in (2, 1, 3):
        z_copy(d).start()
    for fq in range(3, FQ):
        send_bg(fq)
    total = zsend[z]
    for d in range(1, Z):
        z_arrival(d).wait_recv()
        total = total + zrecv[lax.rem(z + d, Z)]

    system, right_side = unpack_system(total)
    mixing = mixing_t(inverse_root(system), right_side)
    wide = dot(dot(expand, mixing).astype(BF), expand_t)
    same = (iota((4 * K, 4 * K), 0) % 4) == (iota((4 * K, 4 * K), 1) % 4)
    spread = jnp.where(same, wide, 0.0).astype(BF)

    for fq in range(FQ):
        for d in (2, 1, 3):
            bg_arrival(fq, d).wait_recv()
        block = dot(spread, land[fq].reshape(Z * K, PATCH))
        back[fq] = block.astype(BF).reshape(Z, K, PATCH)
        for d in (2, 1, 3):
            back_copy(fq, d).start()

    def place(fq, m, ref):
        cells = pl.ds(pl.multiple_of(m * PATCH, PATCH), PATCH)
        for j in range(FL):
            out[j, 4 * fq : 4 * fq + 4, cells] = ref[fq, m, 4 * j : 4 * j + 4]

    for fq in range(FQ):
        place(fq, z, back)
    for fq in range(FQ):
        for d in (2, 1, 3):
            back_arrival(fq, d).wait_recv()
            place(fq, lax.rem(z + d, Z), back_land)

    for g in range(NG):
        core_copy(g).wait_send()

        def sent(d, carry):
            plane_copy(g, d).wait_send()
            return carry

        lax.fori_loop(1, XY, sent, 0)
    for d in range(1, Z):
        z_copy(d).wait_send()
        for fq in range(FQ):
            bg_copy(fq, d).wait_send()
            back_copy(fq, d).wait_send()


def per_device(background, perturbation, innovation, obs_weight, route_dest, localization):
    sem = pltpu.SemaphoreType.DMA
    scratch = [
        pltpu.VMEM((FL, FL, Z * PATCH), BF),
        pltpu.VMEM((K, OBS), BF),
        pltpu.VMEM((2, OBS), jnp.int32),
        pltpu.VMEM((1, OBS), F32),
        pltpu.VMEM((1, OBS), F32),
        pltpu.VMEM((2, 1, OBS), F32),
        pltpu.VMEM((UNITS, OBS), BF),
        pltpu.VMEM((UNITS, OBS), BF),
        pltpu.VMEM((2, 8 * 128, OBS), BF),
        pltpu.VMEM((NG, 2, 8, 64, 128), F32),
        pltpu.VMEM((NG, 8, 64, 128), F32),
        pltpu.VMEM((NG, 64 * 8, 128), F32),
        pltpu.VMEM((NG, XY, 32, 128), BF),
        pltpu.VMEM((NG, XY, 32, 128), BF),
        pltpu.VMEM((Z, 8 * NG, 128), F32),
        pltpu.VMEM((Z, 8 * NG, 128), F32),
        pltpu.VMEM((FQ, Z - 1, K, PATCH), BF),
        pltpu.VMEM((FQ, Z, K, PATCH), BF),
        pltpu.VMEM((FQ, Z, K, PATCH), BF),
        pltpu.VMEM((FQ, Z, K, PATCH), BF),
        sem((6,)),
        sem((NG,)),
        sem((NG,)),
        sem((NG, XY)),
        sem((NG, XY)),
        sem((Z,)),
        sem((Z,)),
        sem((FQ, Z)),
        sem((FQ, Z)),
        sem((FQ, Z)),
        sem((FQ, Z)),
    ]
    return pl.pallas_call(
        kernel,
        name="analysis",
        out_shape=jax.ShapeDtypeStruct(background.shape, BF),
        in_specs=[pl.BlockSpec(memory_space=pl.ANY)] * 6,
        out_specs=pl.BlockSpec(memory_space=pltpu.VMEM),
        scratch_shapes=scratch,
        compiler_params=pltpu.CompilerParams(collective_id=0, has_side_effects=True, vmem_limit_bytes=52 << 20),
    )(
        background,
        perturbation,
        route_dest.T,
        obs_weight.reshape(1, OBS),
        innovation.reshape(1, OBS),
        localization,
    )


def solution(mesh):
    in_specs = (
        P("member", None, "space"),
        P(None, ("member", "space")),
        P(("member", "space")),
        P(("member", "space")),
        P(("member", "space"), None),
        P(None, None, ("member", "space")),
    )
    out_specs = P("member", None, "space")
    return jax.shard_map(per_device, mesh=mesh, in_specs=in_specs, out_specs=out_specs, check_vma=False)
```

time: 266 us -> 62 us (0.23)
  the two profiles are of different devices: /device:TPU:0 before, /device:TPU:1 now
where the time goes in v1:
time: 62 us; the launch traced here: 61.6 us
  Pallas kernels  54.5 us (88%)
  local copies, waits for them, and re-layouts  7.08 us (11%)
    pallas_call x1, Pallas kernels, per_device(): pl.pallas_call(kernel, name='analysis', out_shape=jax.ShapeDtypeStruct(ba...  54.5 us
    unnamed x11, local copies, waits for them, and re-layouts  7.08 us

profile of v1, /device:TPU:1, one launch (start us, length us, event | category | flops | bytes accessed | tf_op | source)
XLA Modules:
  0.0 61.6 jit_solution(1991838682305107665)
XLA Ops:
  0.0 0.0 copy-start
  0.0 1.1 %copy-done = bf16[80,4096]{1,0:T(8,128)(2,1)S(1)} copy-done((bf16[80,4096]{1,0:T(8,128)(2,1)S(1)}, bf16[80,4096]{1,0:T(8,128)(2,1)}, u32[]{:S(2)}) %copy-start) | copy-done | bytes 655384
  1.1 0.0 copy-start.1
  1.1 0.8 %copy-done.1 = s32[4096,2]{0,1:T(2,128)S(1)} copy-done((s32[4096,2]{0,1:T(2,128)S(1)}, s32[4096,2]{0,1:T(2,128)}, u32[]{:S(2)}) %copy-start.1) | copy-done | bytes 32792
  1.8 0.0 copy-start.2
  1.8 0.8 %copy-done.2 = f32[2,1,4096]{2,1,0:T(1,128)S(1)} copy-done((f32[2,1,4096]{2,1,0:T(1,128)S(1)}, f32[2,1,4096]{2,1,0:T(1,128)}, u32[]{:S(2)}) %copy-start.2) | copy-done | bytes 32792
  2.6 0.0 copy-start.3
  2.6 0.7 %copy-done.3 = f32[4096]{0:T(1024)S(1)} copy-done((f32[4096]{0:T(1024)S(1)}, f32[4096]{0:T(1024)}, u32[]{:S(2)}) %copy-start.3) | copy-done | bytes 16408
  3.3 0.0 copy-start.4
  3.3 0.7 %copy-done.4 = f32[4096]{0:T(1024)S(1)} copy-done((f32[4096]{0:T(1024)S(1)}, f32[4096]{0:T(1024)}, u32[]{:S(2)}) %copy-start.4) | copy-done | bytes 16408
  4.0 54.5 %analysis.1 = bf16[20,20,2048]{2,1,0:T(8,128)(2,1)} custom-call(bf16[20,20,2048]{2,1,0:T(8,128)(2,1)} %bg.1, bf16[80,4096]{1,0:T(8,128)(2,1)S(1)} %copy-done, s32[2,4096]{1,0:T(2,128)S(1)} %bitcast.3, f32[1,4096]{1,0:T(1,128)S(1)} %bitcast.4, f32[1,4096]{1,0:T(1,128)S(1)} %bitcast.5, f32[2,1,4096]{2,1,0:T(1,128)S(1)} %copy-done.2), custom_call_target="tpu_custom_call" | custom-call | tf_op jit(solution)/shard_map/analysis/pallas_call | solution.py:387
  58.5 3.0 %copy.8 = bf16[20,20,2048]{2,1,0:T(8,128)(2,1)} copy(bf16[20,20,2048]{2,1,0:T(8,128)(2,1)} %analysis.1) | data formatting | bytes 3276800
Async XLA Ops:
  0.0 1.1 %copy-start = (bf16[80,4096]{1,0:T(8,128)(2,1)S(1)}, bf16[80,4096]{1,0:T(8,128)(2,1)}, u32[]{:S(2)}) copy-start(bf16[80,4096]{1,0:T(8,128)(2,1)} %y_in.1) | copy-start | bytes 1966084
  1.1 0.8 %copy-start.1 = (s32[4096,2]{0,1:T(2,128)S(1)}, s32[4096,2]{0,1:T(2,128)}, u32[]{:S(2)}) copy-start(s32[4096,2]{0,1:T(2,128)} %param.10) | copy-start | bytes 98308
  1.8 0.8 %copy-start.2 = (f32[2,1,4096]{2,1,0:T(1,128)S(1)}, f32[2,1,4096]{2,1,0:T(1,128)}, u32[]{:S(2)}) copy-start(f32[2,1,4096]{2,1,0:T(1,128)} %local_in.1) | copy-start | bytes 98308
  2.6 0.7 %copy-start.3 = (f32[4096]{0:T(1024)S(1)}, f32[4096]{0:T(1024)}, u32[]{:S(2)}) copy-start(f32[4096]{0:T(1024)} %param.9) | copy-start | bytes 49156
  3.3 0.7 %copy-start.4 = (f32[4096]{0:T(1024)S(1)}, f32[4096]{0:T(1024)}, u32[]{:S(2)}) copy-start(f32[4096]{0:T(1024)} %param.8) | copy-start | bytes 49156

commit v2 on v1

v2 whole, which is shorter than its diff:
```python
import math

import jax
import jax.numpy as jnp
from jax import lax
from jax.experimental import pallas as pl
from jax.experimental.pallas import tpu as pltpu
from jax.sharding import PartitionSpec as P

BF = jnp.bfloat16
F32 = jnp.float32
MESH = pl.DeviceIdType.MESH
NN = (((1,), (0,)), ((), ()))
NT = (((1,), (1,)), ((), ()))

K = 80
OBS = 4096
UNITS = 128
Z = 4
XY = 16
HALF = UNITS // 2
FL = 20
FQ = 5
PATCH = 512
NS_STEPS = 8
VMEM_LIMIT = 63 << 20

GROUPS = (
    ((0, 0, 80), (32, 32, 48)),
    ((8, 8, 72), (24, 24, 56)),
    ((16, 16, 64), (40, 40, 40), (56, 56, 24)),
    ((48, 48, 32), (64, 64, 16), (72, 72, 8)),
)
NG = len(GROUPS)
WIDTH = tuple(sum(n for _, _, n in blocks) for blocks in GROUPS)
RHS_LANE = WIDTH[-1]


def iota(shape, dim):
    return lax.broadcasted_iota(jnp.int32, shape, dim)


def dot(a, b, dims=NN, precision=None):
    return lax.dot_general(a, b, dims, preferred_element_type=F32, precision=precision)


def dot_exact(a, b):
    return dot(a, b, precision=lax.Precision.HIGHEST)


def build_weights(dest, weight, innovation, localization, coef, weighted):
    step = 512
    row = iota((UNITS, 1), 0)
    unit = (row % Z) * 32 + ((row % HALF) // Z) * 2 + row // HALF
    for start in range(0, OBS, step):
        at = slice(start, start + step)
        first = weight[:, at] * localization[0, :, at]
        second = weight[:, at] * localization[1, :, at]
        to_first = dest[0:1, at] == unit
        to_second = dest[1:2, at] == unit

        def pick(a, b):
            a, b = a.astype(BF).astype(F32), b.astype(BF).astype(F32)
            return jnp.where(to_first, a, jnp.where(to_second, b, 0.0)).astype(BF)

        coef[:, at] = pick(first, second)
        weighted[:, at] = pick(first * innovation[:, at], second * innovation[:, at])


def build_products(y, feats, group):
    step = 512
    for start in range(0, OBS, step):
        at = slice(start, start + step)
        row = 0
        for i in range(8):
            for k, l, n in GROUPS[group]:
                feats[row : row + n, at] = y[k + i : k + i + 1, at] * y[l : l + n, at]
                row += n


def inverse_root(system):
    eye = (iota((K, K), 0) == iota((K, K), 1)).astype(F32)
    upper = jnp.max(jnp.sum(jnp.abs(system), axis=1, keepdims=True), axis=0, keepdims=True)
    low = jnp.sqrt((K - 1.0) / upper)
    approx, inverse = system * (1.0 / upper), None
    for step in range(NS_STEPS):
        square = 3.0 / (1.0 + low + low * low)
        stretch = jnp.sqrt(square)
        product = approx if inverse is None else dot_exact(inverse, approx)
        half = (1.5 * stretch) * eye - (0.5 * stretch * square) * product
        low = 0.5 * stretch * low * (3.0 - square * low * low)
        if step < NS_STEPS - 1:
            approx = dot_exact(approx, half)
        inverse = half if inverse is None else dot_exact(half, inverse)
    return inverse * lax.rsqrt(upper)


def unpack_system(total):
    lane = iota((8, 128), 1)
    tiles = [None] * (K // 8)
    for g, blocks in enumerate(GROUPS):
        slots = total[8 * g : 8 * g + 8]
        offset = 0
        for k, l, n in blocks:
            rolled = pltpu.roll(slots, (l - offset) % 128, 1) if l != offset else slots
            tiles[k // 8] = jnp.where((lane >= l) & (lane < l + n), rolled, 0.0)
            offset += n
    upper = jnp.concatenate(tiles + [jnp.zeros((128 - K, 128), F32)], axis=0)
    row, col = iota((128, 128), 0), iota((128, 128), 1)
    above = jnp.where((row // 8) == (col // 8), 0.0, upper)
    gram = (upper + above.T)[:K, :K]
    eye = (iota((K, K), 0) == iota((K, K), 1)).astype(F32)
    slots = total[8 * (NG - 1) :]
    part = jnp.zeros((8, 128), F32)
    for i in range(K // 16):
        rolled = pltpu.roll(slots, (16 * i - RHS_LANE) % 128, 1) + pltpu.roll(slots, (16 * i - RHS_LANE - 16) % 128, 1)
        part = jnp.where((iota((8, 128), 0) == i) & (lane // 16 == i), rolled, part)
    right_side = jnp.sum(part, axis=0, keepdims=True)[:, :K]
    return gram + (K - 1.0) * eye, right_side


def mixing_t(root, right_side):
    halfway = jnp.sum(root * right_side, axis=1, keepdims=True)
    mean = jnp.sum(root * halfway, axis=0, keepdims=True)
    spread = math.sqrt(K - 1.0) * root
    column = jnp.sum(mean, axis=1, keepdims=True) + jnp.sum(spread, axis=1, keepdims=True)
    return (mean + spread + (1.0 - column) / K).astype(BF)


def kernel(
    bg, y_in, dest_in, weight_in, innovation_in, local_in, out,
    bgv, y, dest, weight, innovation, local, coef, weighted, feats,
    stage, peer_stage, stage16, plane, zsend, zrecv, prep, land, back,
    in_sem, core_s, core_r, plane_s, plane_r, z_s, z_r, bg_s, bg_r, back_s, back_r, own_s,
):
    z = lax.axis_index("member")
    s = lax.axis_index("space")
    core = lax.rem(s, 2)
    xy = lax.div(s, 2)

    def z_peer(d):
        return (lax.rem(z + d, Z), s)

    def plane_chip(d):
        return lax.rem(lax.div(xy, 4) + d // 4, 4) * 4 + lax.rem(lax.rem(xy, 4) + d % 4, 4)

    def plane_peer(d):
        return (z, 2 * plane_chip(d) + core)

    core_peer = (z, 2 * xy + 1 - core)

    barrier = pltpu.get_barrier_semaphore()
    far_first = sorted(range(1, XY), key=lambda d: -(min(d // 4, 4 - d // 4) + min(d % 4, 4 - d % 4)))
    peers = [plane_peer(d) for d in far_first] + [z_peer(d) for d in (2, 1, 3)] + [core_peer]
    for peer in peers:
        pl.semaphore_signal(barrier, inc=1, device_id=peer, device_id_type=MESH)

    loads = [
        pltpu.make_async_copy(src, dst, in_sem.at[i])
        for i, (src, dst) in enumerate(
            ((dest_in, dest), (weight_in, weight), (local_in, local), (innovation_in, innovation), (y_in, y), (bg, bgv))
        )
    ]
    for load in loads:
        load.start()

    def remote(src, dst, send, recv, peer):
        return pltpu.make_async_remote_copy(src, dst, send, recv, device_id=peer, device_id_type=MESH)

    branch = pl.when(z >= 0)

    def send_bg(*fqs):
        @branch
        def _():
            for fq in fqs:
                send_bg_group(fq)

    def send_bg_group(fq):
        for d in (2, 1, 3):
            remote(prep.at[fq, d - 1], land.at[fq, z], bg_s, bg_r.at[fq], z_peer(d)).start()

    def bg_arrivals(fq):
        return remote(prep.at[fq], land.at[fq, 0 : Z - 1], bg_s, bg_r.at[fq], z_peer(1))

    def bg_sends():
        return remote(prep, prep, bg_s, bg_r.at[0], z_peer(1))

    def core_copy(g):
        return remote(stage.at[g, 1 - core], peer_stage.at[g], core_s.at[g], core_r.at[g], core_peer)

    def send_core(g):
        @branch
        def _():
            core_copy(g).start()

    def send_plane(g):
        core_copy(g).wait_recv()
        total = stage[g, core] + peer_stage[g]
        if g == NG - 1:
            rest = pltpu.roll(total - total.astype(BF).astype(F32), 16, 1)
            lane = iota(total.shape, 1)
            total = jnp.where((lane >= RHS_LANE + 16) & (lane < RHS_LANE + 32), rest, total)
        stage16[g] = total.reshape(XY, 8 * Z, 128).astype(BF)

        @branch
        def _():
            for d in far_first:
                remote(stage16.at[g, plane_chip(d)], plane.at[g, d - 1], plane_s.at[g], plane_r.at[g], plane_peer(d)).start()

    def plane_all(g):
        return remote(plane.at[g], plane.at[g], plane_s.at[g], plane_r.at[g], plane_peer(1))

    def send_column():
        @branch
        def _():
            for d in (2, 1, 3):
                remote(zsend.at[lax.rem(z + d, Z)], zrecv.at[d - 1], z_s, z_r, z_peer(d)).start()

    def column_all():
        return remote(zrecv, zrecv, z_s, z_r, z_peer(1))

    def send_back(fq):
        @branch
        def _():
            for d in (2, 1, 3):
                remote(back.at[fq, lax.rem(z + d, Z)], out.at[fq, z], back_s, back_r, z_peer(d)).start()
            own_copy(fq).start()

    def back_all():
        return remote(back.at[:, 0 : Z - 1], out.at[:, 0 : Z - 1], back_s, back_r, z_peer(1))

    def own_all():
        return pltpu.make_async_copy(back.at[:, 0], out.at[:, 0], own_s)

    def own_copy(fq):
        return pltpu.make_async_copy(back.at[fq, z], out.at[fq, z], own_s)

    def partial_gram(g):
        width = WIDTH[g]
        buf = feats.at[g % 2]
        build_products(y, buf, g)
        tail = None
        if g == NG - 1:
            tail = dot(y[...], weighted[...], NT)
        for part in range(2):
            rows = 4 * width
            result = dot(buf[part * rows : (part + 1) * rows, :], coef[...], NT)
            for j in range(4):
                i = 4 * part + j
                slot = result[j * width : (j + 1) * width]
                if width < 128:
                    pieces = [slot]
                    filled = width
                    if i < K // 16:
                        pieces.append(tail[16 * i : 16 * i + 16])
                        filled += 16
                    pieces.append(jnp.zeros((128 - filled, UNITS), F32))
                    slot = jnp.concatenate(pieces, axis=0)
                turned = slot.T
                stage[g, 0, pl.ds(i, HALF, stride=8), :] = turned[:HALF]
                stage[g, 1, pl.ds(i, HALF, stride=8), :] = turned[HALF:]

    def sum_plane(g):
        plane_all(g).wait_recv()
        total = stage16[g, xy].astype(F32)
        for d in range(XY - 1):
            total = total + plane[g, d].astype(F32)
        for t in range(Z):
            zsend[t, 8 * g : 8 * g + 8] = total[8 * t : 8 * t + 8]

    for load in loads[:4]:
        load.wait()
    build_weights(dest, weight, innovation, local, coef, weighted)
    loads[4].wait()
    partial_gram(0)
    loads[5].wait()
    for fq in range(FQ):
        rows = slice(4 * fq, 4 * fq + 4)
        for j in range(FL):
            to = slice(4 * j, 4 * j + 4)
            land[fq, z, to] = bgv[j, rows, pl.ds(pl.multiple_of(z * PATCH, PATCH), PATCH)]
            for d in range(1, Z):
                cells = pl.ds(pl.multiple_of(lax.rem(z + d, Z) * PATCH, PATCH), PATCH)
                prep[fq, d - 1, to] = bgv[j, rows, cells]

    pl.semaphore_wait(barrier, len(peers))
    send_core(0)
    send_bg(0, 1, 2)
    for g in range(1, NG):
        partial_gram(g)
        send_core(g)
        send_plane(g - 1)
    send_plane(NG - 1)
    expand_t = (iota((K, 4 * K), 0) == (iota((K, 4 * K), 1) // 4)).astype(BF)
    for g in range(NG):
        sum_plane(g)
    send_column()
    send_bg(3, 4)
    total = zsend[z]
    column_all().wait_recv()
    for d in range(Z - 1):
        total = total + zrecv[d]

    system, right_side = unpack_system(total)
    mixing = mixing_t(inverse_root(system), right_side)
    wide = jnp.broadcast_to(dot(mixing, expand_t)[:, None, :], (K, 4, 4 * K)).reshape(4 * K, 4 * K)
    same = (iota((4 * K, 4 * K), 0) % 4) == (iota((4 * K, 4 * K), 1) % 4)
    spread = jnp.where(same, wide, 0.0).astype(BF)

    for fq in range(FQ):
        bg_arrivals(fq).wait_recv()
        block = dot(spread, land[fq].reshape(Z * K, PATCH))
        back[fq] = block.astype(BF).reshape(Z, K, PATCH)
        send_back(fq)

    for g in range(NG):
        core_copy(g).wait_send()
        plane_all(g).wait_send()
    column_all().wait_send()
    bg_sends().wait_send()
    own_all().wait()
    back_all().wait()


def unpack(dense, out, piece, whole, load_sem, store_sem):
    loads = [pltpu.make_async_copy(dense.at[:, m], piece.at[:, m], load_sem.at[m]) for m in range(Z)]
    for load in loads:
        load.start()
    stores = []
    for m in range(Z):
        loads[m].wait()
        cells = slice(m * PATCH, (m + 1) * PATCH)
        for fq in range(FQ):
            for j in range(FL):
                whole[j, 4 * fq : 4 * fq + 4, cells] = piece[fq, m, 4 * j : 4 * j + 4]
        stores.append(pltpu.make_async_copy(whole.at[:, :, cells], out.at[:, :, cells], store_sem.at[m]))
        stores[-1].start()
    for store in stores:
        store.wait()


def per_device(background, perturbation, innovation, obs_weight, route_dest, localization):
    sem = pltpu.SemaphoreType.DMA
    scratch = [
        pltpu.VMEM((FL, FL, Z * PATCH), BF),
        pltpu.VMEM((K, OBS), BF),
        pltpu.VMEM((2, OBS), jnp.int32),
        pltpu.VMEM((1, OBS), F32),
        pltpu.VMEM((1, OBS), F32),
        pltpu.VMEM((2, 1, OBS), F32),
        pltpu.VMEM((UNITS, OBS), BF),
        pltpu.VMEM((UNITS, OBS), BF),
        pltpu.VMEM((2, 8 * 128, OBS), BF),
        pltpu.VMEM((NG, 2, HALF * 8, 128), F32),
        pltpu.VMEM((NG, HALF * 8, 128), F32),
        pltpu.VMEM((NG, XY, 8 * Z, 128), BF),
        pltpu.VMEM((NG, XY - 1, 8 * Z, 128), BF),
        pltpu.VMEM((Z, 8 * NG, 128), F32),
        pltpu.VMEM((Z - 1, 8 * NG, 128), F32),
        pltpu.VMEM((FQ, Z - 1, K, PATCH), BF),
        pltpu.VMEM((FQ, Z, K, PATCH), BF),
        pltpu.VMEM((FQ, Z, K, PATCH), BF),
        sem((6,)),
        sem((NG,)),
        sem((NG,)),
        sem((NG,)),
        sem((NG,)),
        sem,
        sem,
        sem,
        sem((FQ,)),
        sem,
        sem,
        sem,
    ]
    analysed = pl.pallas_call(
        kernel,
        name="analysis",
        out_shape=jax.ShapeDtypeStruct((FQ, Z, K, PATCH), BF),
        in_specs=[pl.BlockSpec(memory_space=pl.ANY)] * 6,
        out_specs=pl.BlockSpec(memory_space=pl.ANY),
        scratch_shapes=scratch,
        compiler_params=pltpu.CompilerParams(collective_id=0, has_side_effects=True, vmem_limit_bytes=VMEM_LIMIT),
    )(
        background,
        perturbation,
        route_dest.T,
        obs_weight.reshape(1, OBS),
        innovation.reshape(1, OBS),
        localization,
    )
    return pl.pallas_call(
        unpack,
        name="unpack",
        out_shape=jax.ShapeDtypeStruct(background.shape, BF),
        in_specs=[pl.BlockSpec(memory_space=pl.ANY)],
        out_specs=pl.BlockSpec(memory_space=pl.ANY),
        scratch_shapes=[
            pltpu.VMEM((FQ, Z, K, PATCH), BF),
            pltpu.VMEM((FL, FL, Z * PATCH), BF),
            sem((Z,)),
            sem((Z,)),
        ],
        compiler_params=pltpu.CompilerParams(vmem_limit_bytes=VMEM_LIMIT),
    )(analysed)


def solution(mesh):
    in_specs = (
        P("member", None, "space"),
        P(None, ("member", "space")),
        P(("member", "space")),
        P(("member", "space")),
        P(("member", "space"), None),
        P(None, None, ("member", "space")),
    )
    out_specs = P("member", None, "space")
    return jax.shard_map(per_device, mesh=mesh, in_specs=in_specs, out_specs=out_specs, check_vma=False)
```

time: 62 us -> 54.3 us (0.88)
  the two profiles are of different devices: /device:TPU:1 before, /device:TPU:0 now
where the time goes in v2:
time: 54.3 us; the launch traced here: 53.2 us
  Pallas kernels  53.1 us (98%)
    pallas_call x1, Pallas kernels, per_device(): pl.pallas_call(kernel, name='analysis', out_shape=jax.ShapeDtypeStruct((F...  50.6 us
    pallas_call x1, Pallas kernels, per_device(): pl.pallas_call(unpack, name='unpack', out_shape=jax.ShapeDtypeStruct(back...  2.42 us

profile of v2, /device:TPU:0, one launch (start us, length us, event | category | flops | bytes accessed | tf_op | source)
XLA Modules:
  0.0 53.2 jit_solution(1498070192993203460)
XLA Ops:
  0.0 50.6 %analysis.1.dense = bf16[5,4,80,512]{3,2,1,0:T(8,128)(2,1)} custom-call(bf16[20,20,2048]{2,1,0:T(8,128)(2,1)} %bg.1, bf16[80,4096]{1,0:T(8,128)(2,1)} %y_in.1, s32[2,4096]{1,0:T(2,128)} %bitcast.3, f32[1,4096]{1,0:T(1,128)} %bitcast.4, f32[1,4096]{1,0:T(1,128)} %bitcast.5, f32[2,1,4096]{2,1,0:T(1,128)} %local_in.1), custom_call_target="tpu_custom_call" | custom-call | tf_op jit(solution)/shard_map/analysis/pallas_call | solution.py:376
  50.6 2.4 %unpack.1 = bf16[20,20,2048]{2,1,0:T(8,128)(2,1)} custom-call(bf16[5,4,80,512]{3,2,1,0:T(8,128)(2,1)} %analysis.1.dense), custom_call_target="tpu_custom_call" | custom-call | tf_op jit(solution)/shard_map/unpack/pallas_call | solution.py:392

commit v3 on v2

--- a/solution.py
+++ b/solution.py
@@ -23,6 +23,8 @@
 FQ = 5
 PATCH = 512
 NS_STEPS = 8
+BG_PARTS = ((0, 4), (4, FQ))
+BACK_PARTS = ((0, 1), (1, 3), (3, FQ))
 VMEM_LIMIT = 63 << 20
 
 GROUPS = (
@@ -149,12 +151,6 @@
 
     core_peer = (z, 2 * xy + 1 - core)
 
-    barrier = pltpu.get_barrier_semaphore()
-    far_first = sorted(range(1, XY), key=lambda d: -(min(d // 4, 4 - d // 4) + min(d % 4, 4 - d % 4)))
-    peers = [plane_peer(d) for d in far_first] + [z_peer(d) for d in (2, 1, 3)] + [core_peer]
-    for peer in peers:
-        pl.semaphore_signal(barrier, inc=1, device_id=peer, device_id_type=MESH)
-
     loads = [
         pltpu.make_async_copy(src, dst, in_sem.at[i])
         for i, (src, dst) in enumerate(
@@ -164,23 +160,29 @@
     for load in loads:
         load.start()
 
+    barrier = pltpu.get_barrier_semaphore()
+    far_first = sorted(range(1, XY), key=lambda d: -(min(d // 4, 4 - d // 4) + min(d % 4, 4 - d % 4)))
+    peers = [plane_peer(d) for d in far_first] + [z_peer(d) for d in (2, 1, 3)] + [core_peer]
+    for peer in peers:
+        pl.semaphore_signal(barrier, inc=1, device_id=peer, device_id_type=MESH)
+
+
     def remote(src, dst, send, recv, peer):
         return pltpu.make_async_remote_copy(src, dst, send, recv, device_id=peer, device_id_type=MESH)
 
     branch = pl.when(z >= 0)
 
-    def send_bg(*fqs):
+    def send_bg(part):
+        fqs = slice(*BG_PARTS[part])
+
         @branch
         def _():
-            for fq in fqs:
-                send_bg_group(fq)
-
-    def send_bg_group(fq):
-        for d in (2, 1, 3):
-            remote(prep.at[fq, d - 1], land.at[fq, z], bg_s, bg_r.at[fq], z_peer(d)).start()
-
-    def bg_arrivals(fq):
-        return remote(prep.at[fq], land.at[fq, 0 : Z - 1], bg_s, bg_r.at[fq], z_peer(1))
+            for d in (2, 1, 3):
+                remote(prep.at[fqs, d - 1], land.at[fqs, z], bg_s, bg_r.at[part], z_peer(d)).start()
+
+    def bg_arrivals(part):
+        fqs = slice(*BG_PARTS[part])
+        return remote(prep.at[fqs], land.at[fqs, 0 : Z - 1], bg_s, bg_r.at[part], z_peer(1))
 
     def bg_sends():
         return remote(prep, prep, bg_s, bg_r.at[0], z_peer(1))
@@ -219,12 +221,17 @@
     def column_all():
         return remote(zrecv, zrecv, z_s, z_r, z_peer(1))
 
-    def send_back(fq):
+    def own_copy(fqs):
+        return pltpu.make_async_copy(back.at[fqs, z], out.at[fqs, z], own_s)
+
+    def send_back(part):
+        fqs = slice(*BACK_PARTS[part])
+
         @branch
         def _():
             for d in (2, 1, 3):
-                remote(back.at[fq, lax.rem(z + d, Z)], out.at[fq, z], back_s, back_r, z_peer(d)).start()
-            own_copy(fq).start()
+                remote(back.at[fqs, lax.rem(z + d, Z)], out.at[fqs, z], back_s, back_r, z_peer(d)).start()
+            own_copy(fqs).start()
 
     def back_all():
         return remote(back.at[:, 0 : Z - 1], out.at[:, 0 : Z - 1], back_s, back_r, z_peer(1))
@@ -232,17 +239,15 @@
     def own_all():
         return pltpu.make_async_copy(back.at[:, 0], out.at[:, 0], own_s)
 
-    def own_copy(fq):
-        return pltpu.make_async_copy(back.at[fq, z], out.at[fq, z], own_s)
-
-    def partial_gram(g):
+    def partial_gram(g, parts=(0, 1)):
         width = WIDTH[g]
         buf = feats.at[g % 2]
-        build_products(y, buf, g)
+        if 0 in parts:
+            build_products(y, buf, g)
         tail = None
         if g == NG - 1:
             tail = dot(y[...], weighted[...], NT)
-        for part in range(2):
+        for part in parts:
             rows = 4 * width
             result = dot(buf[part * rows : (part + 1) * rows, :], coef[...], NT)
             for j in range(4):
@@ -285,7 +290,7 @@
 
     pl.semaphore_wait(barrier, len(peers))
     send_core(0)
-    send_bg(0, 1, 2)
+    send_bg(0)
     for g in range(1, NG):
         partial_gram(g)
         send_core(g)
@@ -295,7 +300,7 @@
     for g in range(NG):
         sum_plane(g)
     send_column()
-    send_bg(3, 4)
+    send_bg(1)
     total = zsend[z]
     column_all().wait_recv()
     for d in range(Z - 1):
@@ -307,11 +312,14 @@
     same = (iota((4 * K, 4 * K), 0) % 4) == (iota((4 * K, 4 * K), 1) % 4)
     spread = jnp.where(same, wide, 0.0).astype(BF)
 
-    for fq in range(FQ):
-        bg_arrivals(fq).wait_recv()
-        block = dot(spread, land[fq].reshape(Z * K, PATCH))
-        back[fq] = block.astype(BF).reshape(Z, K, PATCH)
-        send_back(fq)
+    bg_arrivals(0).wait_recv()
+    for part, (first, last) in enumerate(BACK_PARTS):
+        if last == FQ:
+            bg_arrivals(1).wait_recv()
+        for fq in range(first, last):
+            block = dot(spread, land[fq].reshape(Z * K, PATCH))
+            back[fq] = block.astype(BF).reshape(Z, K, PATCH)
+        send_back(part)
 
     for g in range(NG):
         core_copy(g).wait_send()
@@ -368,7 +376,7 @@
         sem,
         sem,
         sem,
-        sem((FQ,)),
+        sem((len(BG_PARTS),)),
         sem,
         sem,
         sem,

time: 54.3 us -> 51.3 us (0.945); the launches traced: 53.2 us -> 51.1 us
  Pallas kernels: 53.1 us -> 50.9 us
    pallas_call x1, Pallas kernels: 50.6 us -> 48.5 us  [per_device(): pl.pallas_call(kernel, name='analysis', out_shape=jax.ShapeDtypeStruct((F...]
where the time goes in v3:
time: 51.3 us; the launch traced here: 51.1 us
  Pallas kernels  50.9 us (99%)
    pallas_call x1, Pallas kernels, per_device(): pl.pallas_call(kernel, name='analysis', out_shape=jax.ShapeDtypeStruct((F...  48.5 us
    pallas_call x1, Pallas kernels, per_device(): pl.pallas_call(unpack, name='unpack', out_shape=jax.ShapeDtypeStruct(back...  2.42 us

profile of v3, /device:TPU:0, one launch (start us, length us, event | category | flops | bytes accessed | tf_op | source)
XLA Modules:
  0.0 51.1 jit_solution(6427867644697865172)
XLA Ops:
  0.0 48.5 %analysis.1.dense = bf16[5,4,80,512]{3,2,1,0:T(8,128)(2,1)} custom-call(bf16[20,20,2048]{2,1,0:T(8,128)(2,1)} %bg.1, bf16[80,4096]{1,0:T(8,128)(2,1)} %y_in.1, s32[2,4096]{1,0:T(2,128)} %bitcast.3, f32[1,4096]{1,0:T(1,128)} %bitcast.4, f32[1,4096]{1,0:T(1,128)} %bitcast.5, f32[2,1,4096]{2,1,0:T(1,128)} %local_in.1), custom_call_target="tpu_custom_call" | custom-call | tf_op jit(solution)/shard_map/analysis/pallas_call | solution.py:384
  48.5 2.4 %unpack.1 = bf16[20,20,2048]{2,1,0:T(8,128)(2,1)} custom-call(bf16[5,4,80,512]{3,2,1,0:T(8,128)(2,1)} %analysis.1.dense), custom_call_target="tpu_custom_call" | custom-call | tf_op jit(solution)/shard_map/unpack/pallas_call | solution.py:400

commit v4 on v3

--- a/solution.py
+++ b/solution.py
@@ -46,11 +46,15 @@
     return lax.dot_general(a, b, dims, preferred_element_type=F32, precision=precision)
 
 
-def dot_exact(a, b):
-    return dot(a, b, precision=lax.Precision.HIGHEST)
-
-
-def build_weights(dest, weight, innovation, localization, coef, weighted):
+def dot_split(a, b):
+    a_high, b_high = a.astype(BF), b.astype(BF)
+    a_low, b_low = (a - a_high.astype(F32)).astype(BF), (b - b_high.astype(F32)).astype(BF)
+    stacked = dot(jnp.concatenate([a_high, a_low], axis=0), b_high)
+    rows = a.shape[0]
+    return stacked[:rows] + (dot(a_high, b_low) + stacked[rows:])
+
+
+def build_weights(dest, weight, localization, innovation, target):
     step = 512
     row = iota((UNITS, 1), 0)
     unit = (row % Z) * 32 + ((row % HALF) // Z) * 2 + row // HALF
@@ -58,15 +62,11 @@
         at = slice(start, start + step)
         first = weight[:, at] * localization[0, :, at]
         second = weight[:, at] * localization[1, :, at]
-        to_first = dest[0:1, at] == unit
-        to_second = dest[1:2, at] == unit
-
-        def pick(a, b):
-            a, b = a.astype(BF).astype(F32), b.astype(BF).astype(F32)
-            return jnp.where(to_first, a, jnp.where(to_second, b, 0.0)).astype(BF)
-
-        coef[:, at] = pick(first, second)
-        weighted[:, at] = pick(first * innovation[:, at], second * innovation[:, at])
+        if innovation is not None:
+            first, second = first * innovation[:, at], second * innovation[:, at]
+        first, second = first.astype(BF).astype(F32), second.astype(BF).astype(F32)
+        chosen = jnp.where(dest[0:1, at] == unit, first, jnp.where(dest[1:2, at] == unit, second, 0.0))
+        target[:, at] = chosen.astype(BF)
 
 
 def build_products(y, feats, group):
@@ -88,12 +88,12 @@
     for step in range(NS_STEPS):
         square = 3.0 / (1.0 + low + low * low)
         stretch = jnp.sqrt(square)
-        product = approx if inverse is None else dot_exact(inverse, approx)
+        product = approx if inverse is None else dot_split(inverse, approx)
         half = (1.5 * stretch) * eye - (0.5 * stretch * square) * product
         low = 0.5 * stretch * low * (3.0 - square * low * low)
         if step < NS_STEPS - 1:
-            approx = dot_exact(approx, half)
-        inverse = half if inverse is None else dot_exact(half, inverse)
+            approx = dot_split(approx, half)
+        inverse = half if inverse is None else dot_split(half, inverse)
     return inverse * lax.rsqrt(upper)
 
 
@@ -125,7 +125,8 @@
     halfway = jnp.sum(root * right_side, axis=1, keepdims=True)
     mean = jnp.sum(root * halfway, axis=0, keepdims=True)
     spread = math.sqrt(K - 1.0) * root
-    column = jnp.sum(mean, axis=1, keepdims=True) + jnp.sum(spread, axis=1, keepdims=True)
+    row_sum = jnp.sum(root, axis=1, keepdims=True)
+    column = jnp.sum(row_sum * halfway, axis=0, keepdims=True) + math.sqrt(K - 1.0) * row_sum
     return (mean + spread + (1.0 - column) / K).astype(BF)
 
 
@@ -239,15 +240,14 @@
     def own_all():
         return pltpu.make_async_copy(back.at[:, 0], out.at[:, 0], own_s)
 
-    def partial_gram(g, parts=(0, 1)):
+    def partial_gram(g):
         width = WIDTH[g]
         buf = feats.at[g % 2]
-        if 0 in parts:
-            build_products(y, buf, g)
+        build_products(y, buf, g)
         tail = None
         if g == NG - 1:
             tail = dot(y[...], weighted[...], NT)
-        for part in parts:
+        for part in range(2):
             rows = 4 * width
             result = dot(buf[part * rows : (part + 1) * rows, :], coef[...], NT)
             for j in range(4):
@@ -275,7 +275,8 @@
 
     for load in loads[:4]:
         load.wait()
-    build_weights(dest, weight, innovation, local, coef, weighted)
+    build_weights(dest, weight, local, None, coef)
+    build_weights(dest, weight, local, innovation, weighted)
     loads[4].wait()
     partial_gram(0)
     loads[5].wait()

time: 51.3 us -> 50.5 us (0.984)
    pallas_call x1, Pallas kernels: 48.5 us -> 47.9 us  [per_device(): pl.pallas_call(kernel, name='analysis', out_shape=jax.ShapeDtypeStruct((F...]
where the time goes in v4:
time: 50.5 us; the launch traced here: 50.4 us
  Pallas kernels  50.4 us (100%)
    pallas_call x1, Pallas kernels, per_device(): pl.pallas_call(kernel, name='analysis', out_shape=jax.ShapeDtypeStruct((F...  47.9 us
    pallas_call x1, Pallas kernels, per_device(): pl.pallas_call(unpack, name='unpack', out_shape=jax.ShapeDtypeStruct(back...  2.42 us

profile of v4, /device:TPU:0, one launch (start us, length us, event | category | flops | bytes accessed | tf_op | source)
XLA Modules:
  0.0 50.4 jit_solution(12177009680199609804)
XLA Ops:
  0.0 47.9 %analysis.1.dense = bf16[5,4,80,512]{3,2,1,0:T(8,128)(2,1)} custom-call(bf16[20,20,2048]{2,1,0:T(8,128)(2,1)} %bg.1, bf16[80,4096]{1,0:T(8,128)(2,1)} %y_in.1, s32[2,4096]{1,0:T(2,128)} %bitcast.3, f32[1,4096]{1,0:T(1,128)} %bitcast.4, f32[1,4096]{1,0:T(1,128)} %bitcast.5, f32[2,1,4096]{2,1,0:T(1,128)} %local_in.1), custom_call_target="tpu_custom_call" | custom-call | tf_op jit(solution)/shard_map/analysis/pallas_call | solution.py:385
  47.9 2.4 %unpack.1 = bf16[20,20,2048]{2,1,0:T(8,128)(2,1)} custom-call(bf16[5,4,80,512]{3,2,1,0:T(8,128)(2,1)} %analysis.1.dense), custom_call_target="tpu_custom_call" | custom-call | tf_op jit(solution)/shard_map/unpack/pallas_call | solution.py:401

commit v5 on v4

--- a/solution.py
+++ b/solution.py
@@ -34,6 +34,7 @@
     ((48, 48, 32), (64, 64, 16), (72, 72, 8)),
 )
 NG = len(GROUPS)
+PLANE_PARTS = ((0, 2), (2, 3), (3, NG))
 WIDTH = tuple(sum(n for _, _, n in blocks) for blocks in GROUPS)
 RHS_LANE = WIDTH[-1]
 
@@ -196,22 +197,28 @@
         def _():
             core_copy(g).start()
 
-    def send_plane(g):
+    def join_cores(g):
         core_copy(g).wait_recv()
         total = stage[g, core] + peer_stage[g]
         if g == NG - 1:
             rest = pltpu.roll(total - total.astype(BF).astype(F32), 16, 1)
             lane = iota(total.shape, 1)
             total = jnp.where((lane >= RHS_LANE + 16) & (lane < RHS_LANE + 32), rest, total)
-        stage16[g] = total.reshape(XY, 8 * Z, 128).astype(BF)
+        stage16[:, g] = total.reshape(XY, 8 * Z, 128).astype(BF)
+
+    def send_plane(part):
+        groups = slice(*PLANE_PARTS[part])
 
         @branch
         def _():
             for d in far_first:
-                remote(stage16.at[g, plane_chip(d)], plane.at[g, d - 1], plane_s.at[g], plane_r.at[g], plane_peer(d)).start()
-
-    def plane_all(g):
-        return remote(plane.at[g], plane.at[g], plane_s.at[g], plane_r.at[g], plane_peer(1))
+                remote(
+                    stage16.at[plane_chip(d), groups], plane.at[d - 1, groups], plane_s.at[part], plane_r.at[part], plane_peer(d)
+                ).start()
+
+    def plane_all(part):
+        arrived = plane.at[:, slice(*PLANE_PARTS[part])]
+        return remote(arrived, arrived, plane_s.at[part], plane_r.at[part], plane_peer(1))
 
     def send_column():
         @branch
@@ -266,10 +273,9 @@
                 stage[g, 1, pl.ds(i, HALF, stride=8), :] = turned[HALF:]
 
     def sum_plane(g):
-        plane_all(g).wait_recv()
-        total = stage16[g, xy].astype(F32)
+        total = stage16[xy, g].astype(F32)
         for d in range(XY - 1):
-            total = total + plane[g, d].astype(F32)
+            total = total + plane[d, g].astype(F32)
         for t in range(Z):
             zsend[t, 8 * g : 8 * g + 8] = total[8 * t : 8 * t + 8]
 
@@ -295,11 +301,17 @@
     for g in range(1, NG):
         partial_gram(g)
         send_core(g)
-        send_plane(g - 1)
-    send_plane(NG - 1)
+        join_cores(g - 1)
+        for part, (_, last) in enumerate(PLANE_PARTS):
+            if last == g:
+                send_plane(part)
+    join_cores(NG - 1)
+    send_plane(len(PLANE_PARTS) - 1)
     expand_t = (iota((K, 4 * K), 0) == (iota((K, 4 * K), 1) // 4)).astype(BF)
-    for g in range(NG):
-        sum_plane(g)
+    for part, (first, last) in enumerate(PLANE_PARTS):
+        plane_all(part).wait_recv()
+        for g in range(first, last):
+            sum_plane(g)
     send_column()
     send_bg(1)
     total = zsend[z]
@@ -324,7 +336,8 @@
 
     for g in range(NG):
         core_copy(g).wait_send()
-        plane_all(g).wait_send()
+    for part in range(len(PLANE_PARTS)):
+        plane_all(part).wait_send()
     column_all().wait_send()
     bg_sends().wait_send()
     own_all().wait()
@@ -362,8 +375,8 @@
         pltpu.VMEM((2, 8 * 128, OBS), BF),
         pltpu.VMEM((NG, 2, HALF * 8, 128), F32),
         pltpu.VMEM((NG, HALF * 8, 128), F32),
-        pltpu.VMEM((NG, XY, 8 * Z, 128), BF),
-        pltpu.VMEM((NG, XY - 1, 8 * Z, 128), BF),
+        pltpu.VMEM((XY, NG, 8 * Z, 128), BF),
+        pltpu.VMEM((XY - 1, NG, 8 * Z, 128), BF),
         pltpu.VMEM((Z, 8 * NG, 128), F32),
         pltpu.VMEM((Z - 1, 8 * NG, 128), F32),
         pltpu.VMEM((FQ, Z - 1, K, PATCH), BF),
@@ -372,8 +385,8 @@
         sem((6,)),
         sem((NG,)),
         sem((NG,)),
-        sem((NG,)),
-        sem((NG,)),
+        sem((len(PLANE_PARTS),)),
+        sem((len(PLANE_PARTS),)),
         sem,
         sem,
         sem,

time: 50.5 us -> 50.7 us (level)
  no operation moved by 1% of the time
where the time goes in v5:
time: 50.7 us; the launch traced here: 50.5 us
  Pallas kernels  50.5 us (100%)
    pallas_call x1, Pallas kernels, per_device(): pl.pallas_call(kernel, name='analysis', out_shape=jax.ShapeDtypeStruct((F...  48.1 us
    pallas_call x1, Pallas kernels, per_device(): pl.pallas_call(unpack, name='unpack', out_shape=jax.ShapeDtypeStruct(back...  2.42 us

profile of v5, /device:TPU:0, one launch (start us, length us, event | category | flops | bytes accessed | tf_op | source)
XLA Modules:
  0.0 50.5 jit_solution(12393974098025201125)
XLA Ops:
  0.0 48.1 %analysis.1.dense = bf16[5,4,80,512]{3,2,1,0:T(8,128)(2,1)} custom-call(bf16[20,20,2048]{2,1,0:T(8,128)(2,1)} %bg.1, bf16[80,4096]{1,0:T(8,128)(2,1)} %y_in.1, s32[2,4096]{1,0:T(2,128)} %bitcast.3, f32[1,4096]{1,0:T(1,128)} %bitcast.4, f32[1,4096]{1,0:T(1,128)} %bitcast.5, f32[2,1,4096]{2,1,0:T(1,128)} %local_in.1), custom_call_target="tpu_custom_call" | custom-call | tf_op jit(solution)/shard_map/analysis/pallas_call | solution.py:398
  48.1 2.4 %unpack.1 = bf16[20,20,2048]{2,1,0:T(8,128)(2,1)} custom-call(bf16[5,4,80,512]{3,2,1,0:T(8,128)(2,1)} %analysis.1.dense), custom_call_target="tpu_custom_call" | custom-call | tf_op jit(solution)/shard_map/unpack/pallas_call | solution.py:414
